TPU v7x, 32 devices: a whole 2x2x4 slice. The times are simulated.
32 devices in a mesh: tile: 8 (over y, x, core), corner: 4 (over z).
Axes of the slice: x: 2, y: 2, z: 4, core: 2. Of those that a mesh axis runs over, the one named last changes fastest.
Arguments:
- mask: float32 [1024, 384], P('tile'), may hold values from 0 to 1
- target: int32 [1024, 384], P('tile'), may hold values 0 or 1
- pixel_weight: float32 [1024, 384], P('tile'), may hold values from 0.49 to 108
- row_taps: float32 [4, 8, 2, 129], replicated, may hold values from -2 to 2
- col_taps: float32 [4, 8, 2, 129], replicated, may hold values from -2 to 2
- kernel_weights: float32 [4, 8], replicated, may hold values from 0.03 to 0.25
- corner_set: int32 [16], P('corner'), may hold values from 0 to 3
- dose: float32 [16], P('corner'), may hold values from 0.8 to 1.25
Outputs:
- soft_error: float32 [1024, 384], P('tile')
- new_mask: float32 [1024, 384], P(('tile', 'corner'))
Inputs may be any that keep to these rules, and one draw needn't show every extreme that they name: `corner_set`: each corner names one of 4 focus settings. target pixels are 0 or 1.
All inputs are finite; a program needn't handle non-finite values. No bound on the sum of `target` on one device may be relied on, other than what follows from the above.
Results may differ from a plain program's by a relative error of at most 0.0051.
Values may be sent and summed in bfloat16 or wider, within the bound.
A program may use at most 64 MiB of HBM per device.

v0:
```python
import jax
import jax.numpy as jnp
from jax import lax
from jax.sharding import PartitionSpec as P

block_cols = 128
lse_sharp = 6.0
print_steep = 3.0
print_level = 1.0
step_rate = 0.25
small_eps = 1e-06


def with_halo(value, sides, width):
    for axis, dim in sides:
        count, length = (lax.axis_size(axis), value.shape[dim])
        up = [(i, (i + 1) % count) for i in range(count - 1)]
        down = [(j, i) for i, j in up]
        last = lax.slice_in_dim(value, length - width, length, axis=dim)
        leading = lax.slice_in_dim(value, 0, width, axis=dim)
        before = lax.ppermute(last, axis, up)
        after = lax.ppermute(leading, axis, down)
        value = jnp.concatenate([before, value, after], axis=dim)
    return value


def passed_along(value, axis, steps):
    count = lax.axis_size(axis)
    leading, last = (max(0, -steps), min(count, count - steps))
    return lax.ppermute(value, axis, [(source, source + steps) for source in range(leading, last)])


def toeplitz(tap_values, row_count):
    leading = tap_values.shape[:-1]
    span_width = row_count + tap_values.shape[-1] - 1
    padded = jnp.concatenate(
        [tap_values, jnp.zeros(leading + (row_count,), tap_values.dtype)], axis=-1
    )
    repeated = jnp.tile(padded, (1,) * len(leading) + (row_count,))
    return repeated[..., : row_count * span_width].reshape(leading + (row_count, span_width))


def column_filter(masked, band_matrix):
    reach_cols = (band_matrix.shape[-1] - block_cols) // 2
    col_count = masked.shape[1]
    padded = jnp.pad(masked, ((0, 0), (reach_cols, reach_cols)))
    windows = jnp.stack(
        [
            padded[:, b * block_cols : b * block_cols + block_cols + 2 * reach_cols]
            for b in range(col_count // block_cols)
        ],
        axis=0,
    )
    product = jnp.einsum("bri,poi->prbo", windows, band_matrix, preferred_element_type=jnp.float32)
    return product.reshape(2, masked.shape[0], col_count)


def row_filter(band_matrix, cfield):
    product = jnp.einsum("aij,bjx->abix", band_matrix, cfield, preferred_element_type=jnp.float32)
    return (product[0, 0] - product[1, 1], product[0, 1] + product[1, 0])


def row_adjoint(band_matrix, cotangent):
    product = jnp.einsum(
        "aij,bix->abjx", band_matrix, cotangent, preferred_element_type=jnp.float32
    )
    return jnp.stack([product[0, 0] + product[1, 1], product[0, 1] - product[1, 0]])


def column_adjoint(back_field, band_matrix):
    reach_cols = (band_matrix.shape[-1] - block_cols) // 2
    line_count = back_field.shape[1]
    col_count = back_field.shape[2]
    blocks = back_field.reshape(2, line_count, col_count // block_cols, block_cols)
    pieces = jnp.einsum("prbo,poi->bri", blocks, band_matrix, preferred_element_type=jnp.float32)
    summed = jnp.zeros((line_count, col_count + 2 * reach_cols), jnp.float32)
    for b in range(col_count // block_cols):
        summed = summed.at[:, b * block_cols : b * block_cols + block_cols + 2 * reach_cols].add(
            pieces[b]
        )
    return summed[:, reach_cols : reach_cols + col_count]


def local(mask, target, pixel_weight, row_taps, col_taps, kernel_weights, corner_set, dose):
    row_count, col_count = mask.shape
    reach_rows = (row_taps.shape[-1] - 1) // 2
    set_count = row_taps.shape[0]
    masked = mask.astype(jnp.bfloat16)
    extended = with_halo(masked, (("tile", 0),), reach_rows)
    target_value = target.astype(jnp.float32)
    exp_total = jnp.zeros((row_count, col_count), jnp.float32)
    corner_states = []
    for c in range(corner_set.shape[0]):
        chosen = (jnp.arange(set_count, dtype=jnp.int32) == corner_set[c]).astype(jnp.float32)
        row_values = jnp.sum(chosen[:, None, None, None] * row_taps, axis=0)
        col_values = jnp.sum(chosen[:, None, None, None] * col_taps, axis=0)
        weights = jnp.sum(chosen[:, None] * kernel_weights, axis=0)
        row_bands = toeplitz(row_values.astype(jnp.bfloat16), row_count)
        col_bands = toeplitz(col_values.astype(jnp.bfloat16), block_cols)

        def forward(running, inputs):
            row_band, col_band, kernel_weight = inputs
            cfield = column_filter(extended, col_band).astype(jnp.bfloat16)
            field_real, field_imag = row_filter(row_band, cfield)
            running = running + kernel_weight * (field_real * field_real + field_imag * field_imag)
            return (running, jnp.stack([field_real, field_imag]).astype(jnp.bfloat16))

        summed, fields = lax.scan(
            forward, jnp.zeros((row_count, col_count), jnp.float32), (row_bands, col_bands, weights)
        )
        intensity = dose[c] * summed
        printed = jax.nn.sigmoid(print_steep * (intensity - print_level))
        differ = printed - target_value
        exp_error = jnp.exp(lse_sharp * (differ * differ))
        exp_total = exp_total + exp_error
        corner_states.append((row_bands, col_bands, weights, fields, printed, exp_error, dose[c]))
    denominator = lax.psum(exp_total.astype(jnp.bfloat16), "corner").astype(jnp.float32)
    soft_error = jnp.log(denominator) / lse_sharp
    grad_ext = jnp.zeros((row_count + 2 * reach_rows, col_count), jnp.float32)
    for corner_state in corner_states:
        row_bands, col_bands, weights, fields, printed, exp_error, corner_dose = corner_state
        slope = (
            pixel_weight
            * (exp_error / denominator)
            * (2.0 * (printed - target_value))
            * printed
            * (1.0 - printed)
            * print_steep
        )
        factor = 2.0 * corner_dose * slope

        def backward(running, inputs):
            row_band, col_band, kernel_weight, field_pair = inputs
            cotangent = (factor * kernel_weight * field_pair).astype(jnp.bfloat16)
            back_field = row_adjoint(row_band, cotangent).astype(jnp.bfloat16)
            return (running + column_adjoint(back_field, col_band), None)

        grad_ext, _ = lax.scan(backward, grad_ext, (row_bands, col_bands, weights, fields))
    upper_rim = grad_ext[:reach_rows]
    lower_rim = grad_ext[row_count + reach_rows :]
    middle = grad_ext[reach_rows : row_count + reach_rows]
    from_below = passed_along(upper_rim, "tile", -1)
    from_above = passed_along(lower_rim, "tile", 1)
    gradient = (
        middle
        + jnp.pad(from_above, ((0, row_count - reach_rows), (0, 0)))
        + jnp.pad(from_below, ((row_count - reach_rows, 0), (0, 0)))
    )
    share_rows = row_count // lax.axis_size("corner")
    first_row = lax.axis_index("corner") * share_rows
    own_mask = lax.dynamic_slice_in_dim(mask, first_row, share_rows, 0)
    pixel_count = row_count * lax.axis_size("tile") * col_count
    summed_grad = lax.psum(gradient, "corner")
    square = lax.psum(jnp.sum(summed_grad * summed_grad), "tile")
    own_rows = lax.dynamic_slice_in_dim(summed_grad, first_row, share_rows, 0)
    root_mean = jnp.sqrt(square / pixel_count + small_eps)
    new_mask = jnp.clip(own_mask - step_rate / root_mean * own_rows, 0.0, 1.0)
    return (soft_error, new_mask)


def solution(mesh):
    placed = (
        P("tile", None),
        P("tile", None),
        P("tile", None),
        P(),
        P(),
        P(),
        P("corner"),
        P("corner"),
    )
    return jax.shard_map(
        local,
        mesh=mesh,
        in_specs=placed,
        out_specs=(P("tile", None), P(("tile", "corner"), None)),
        check_vma=False,
    )
```

profile of v0, /device:TPU:0, one launch (start us, length us, event | category | flops | bytes accessed | tf_op | source)
XLA Modules:
  0.0 593.3 jit_solution(7374306210661256130)
XLA Ops:
  9.4 3.0 collective-permute-start
  27.0 3.1 tile.87
  32.7 3.1 tile.37
  38.4 3.1 tile.39
  44.2 3.1 tile.81
  50.8 3.1 tile.83
  56.5 3.1 tile.33
  62.1 3.1 tile.35
  68.8 49.2 %while.135 = (s32[]{:T(128)}, f32[128,384]{0,1:T(8,128)}, bf16[8,2,128,384]{2,3,0,1:T(8,128)(2,1)}, f32[8]{0:T(128)S(1)}, bf16[8,2,128,256]{3,2,1,0:T(8,128)(2,1...) while((s32[]{:T(128)}, f32[128,384]{0,1:T(8,128)}, ...), condition=%wide.region_19.20_spmd.clone, body=%wide.region_18.19_spmd.clone.sunk | while | flops 203685888 | bytes 5506679 | solution.py:108
  78.1 2.3 bitcast_add_fusion.11
  84.4 2.3 bitcast_add_fusion.11
  90.6 2.3 bitcast_add_fusion.11
  96.9 2.3 bitcast_add_fusion.11
  103.1 2.3 bitcast_add_fusion.11
  109.4 2.3 bitcast_add_fusion.11
  115.6 2.3 bitcast_add_fusion.11
  121.2 49.1 %while.133 = (s32[]{:T(128)}, f32[128,384]{0,1:T(8,128)}, bf16[8,2,128,384]{2,3,0,1:T(8,128)(2,1)}, f32[8]{0:T(128)S(1)}, bf16[8,2,128,256]{3,2,1,0:T(8,128)(2,1...) while((s32[]{:T(128)}, f32[128,384]{0,1:T(8,128)}, ...), condition=%wide.region_9.10_spmd.clone, body=%wide.region_8.9_spmd.clone.sunk | while | flops 203685888 | bytes 5506679 | solution.py:108
  130.5 2.3 bitcast_add_fusion.9
  143.0 2.3 bitcast_add_fusion.9
  149.2 2.3 bitcast_add_fusion.9
  173.5 38.1 %while.134 = (s32[]{:T(128)}, f32[128,384]{0,1:T(8,128)S(1)}, bf16[8,2,128,384]{2,3,0,1:T(8,128)(2,1)}, f32[8]{0:T(128)S(1)}, bf16[8,2,128,256]{3,2,1,0:T(8,128)...) while((s32[]{:T(128)}, f32[128,384]{0,1:T(8,128)S(1)}, ...), condition=%wide.region_14.15_spmd.clone, body=%wide.region_13.14_spmd.clone.sunk | while | flops 203685888 | bytes 5506679 | solution.py:108
  213.8 38.2 %while.132 = (s32[]{:T(128)}, f32[128,384]{0,1:T(8,128)S(1)}, bf16[8,2,128,384]{2,3,0,1:T(8,128)(2,1)}, f32[8]{0:T(128)S(1)}, bf16[8,2,128,256]{3,2,0,1:T(8,128)...) while((s32[]{:T(128)}, f32[128,384]{0,1:T(8,128)S(1)}, ...), condition=%wide.region_4.5_spmd.clone, body=%wide.region_3.4_spmd.clone.sunk | while | flops 203685888 | bytes 5506679 | solution.py:108
  252.1 4.9 add_convert_fusion
  265.0 30.6 %all-reduce.21.cloned.1.call-done = bf16[128,384]{1,0:T(8,128)(2,1)} async-done(((bf16[128,384]{1,0:T(8,128)(2,1)}), bf16[128,384]{1,0:T(8,128)(2,1)}) %all-reduce.21.cloned.1.call-update) | async-done | bytes 98320 | tf_op jit(solution)/shard_map/psum | solution.py:117
  295.5 5.0 fusion.160
  300.6 58.7 %while.136 = (s32[]{:T(128)}, f32[256,384]{0,1:T(8,128)S(1)}, bf16[8,2,128,256]{3,2,0,1:T(8,128)(2,1)}, f32[8]{0:T(128)S(1)}, f32[128,384]{0,1:T(8,128)S(1)}, /*...) while((s32[]{:T(128)}, f32[256,384]{0,1:T(8,128)S(1)}, ...), condition=%wide.region_25.26_spmd.clone, body=%wide.region_23.25_spmd.clone.sunk | while | flops 203374592 | bytes 10618519 | solution.py:138
  360.4 56.3 %while.129 = (s32[]{:T(128)}, f32[256,384]{0,1:T(8,128)S(1)}, bf16[8,2,128,256]{2,3,1,0:T(8,128)(2,1)}, f32[8]{0:T(128)S(1)}, f32[128,384]{0,1:T(8,128)S(1)}, /*...) while((s32[]{:T(128)}, f32[256,384]{0,1:T(8,128)S(1)}, ...), condition=%wide.region_28.29_spmd, body=%wide.region_26.28_spmd.sunk | while | flops 203276288 | bytes 10618501 | solution.py:138
  417.8 57.5 %while.130 = (s32[]{:T(128)}, f32[256,384]{0,1:T(8,128)S(1)}, bf16[8,2,128,256]{2,3,1,0:T(8,128)(2,1)}, f32[8]{0:T(128)S(1)}, f32[128,384]{0,1:T(8,128)S(1)}, /*...) while((s32[]{:T(128)}, f32[256,384]{0,1:T(8,128)S(1)}, ...), condition=%wide.region_31.32_spmd, body=%wide.region_29.31_spmd.sunk | while | flops 203276288 | bytes 10618501 | solution.py:138
  475.4 50.3 %while.131 = (s32[]{:T(128)}, f32[256,384]{0,1:T(8,128)S(1)}, bf16[8,2,128,256]{2,3,1,0:T(8,128)(2,1)S(1)}, f32[8]{0:T(128)S(1)}, f32[128,384]{0,1:T(8,128)S(1)}...) while((s32[]{:T(128)}, f32[256,384]{0,1:T(8,128)S(1)}, ...), condition=%wide.region_34.35_spmd, body=%wide.region_32.34_spmd.sunk | while | flops 203276288 | bytes 10617993 | solution.py:138
  528.5 3.5 collective-permute-done.3
  532.7 37.5 %all-reduce.23.cloned.1.call-done = f32[128,384]{1,0:T(8,128)} async-done(((f32[128,384]{1,0:T(8,128)}), f32[128,384]{1,0:T(8,128)}) %all-reduce.23.cloned.1.call-update) | async-done | bytes 196624 | tf_op jit(solution)/shard_map/psum | solution.py:153
  571.8 12.4 %psum.23 = f32[]{:T(128)} all-reduce(f32[]{:T(128)} %multiply_reduce_fusion), channel_id=1, replica_groups=mesh['tile'=8,'corner'=4] {'tile'}, use_global_device_ids=true, to_apply=%region_37.38 | all-reduce | flops 1 | bytes 8 | tf_op jit(solution)/shard_map/psum | solution.py:154
  (750 shorter events, 430.4 us)
Async XLA Ops:
  7.2 288.4 %all-reduce.21.cloned.1.call-start = ((), (), s32[]{:S(2)}) async-start(), calls=%async_computation | async-start | bytes 196608 | tf_op jit(solution)/shard_map/psum | solution.py:117
  8.2 0.6 copy-start.7
  9.4 57.1 %collective-permute-start = (bf16[64,384]{1,0:T(8,128)(2,1)}, bf16[64,384]{1,0:T(8,128)(2,1)}, u32[]{:S(2)}, u32[]{:S(2)}) collective-permute-start(bf16[64,384]{1,0:T(8,128)(2,1)} %get-tuple-element.1630), channel_id=1, source_target_pairs={{0,4},{4,8},{8,12},{12,16},{16,20},{20,24},{24,28},{1,5},{5,9},{9,... | collective-permute-start | bytes 147464 | tf_op jit(solution)/shard_map/ppermute | solution.py:21
  12.4 54.1 %collective-permute-start.1 = (bf16[64,384]{1,0:T(8,128)(2,1)}, bf16[64,384]{1,0:T(8,128)(2,1)}, u32[]{:S(2)}, u32[]{:S(2)}) collective-permute-start(bf16[64,384]{1,0:T(8,128)(2,1)} %get-tuple-element.1631), channel_id=1, source_target_pairs={{4,0},{8,4},{12,8},{16,12},{20,16},{24,20},{28,24},{5,1},{9,5},{13... | collective-permute-start | bytes 147464 | tf_op jit(solution)/shard_map/ppermute | solution.py:22
  30.1 1.2 copy-start.13
  35.9 1.2 copy-start.12
  41.5 1.3 copy-start.11
  47.3 1.0 copy-start
  48.3 1.2 copy-start.10
  53.9 1.2 copy-start.9
  65.3 1.2 copy-start.8
  118.0 3.2 copy-start.15
  170.3 3.2 copy-start.14
  211.5 2.3 copy-start.16
  252.1 7.0 %copy-start.5 = (f32[128,384]{1,0:T(8,128)}, f32[128,384]{1,0:T(8,128)S(1)}, u32[]{:S(2)}) copy-start(f32[128,384]{1,0:T(8,128)S(1)} %copy.88) | copy-start | bytes 589828
  252.1 9.4 %copy-start.1 = (bf16[8,2,32768]{2,0,1:T(8,128)(2,1)S(1)}, bf16[8,2,32768]{2,0,1:T(8,128)(2,1)}, u32[]{:S(2)}) copy-start(bf16[8,2,32768]{2,0,1:T(8,128)(2,1)} %copy-done) | copy-start | bytes 3145732
  257.1 313.2 %all-reduce.23.cloned.1.call-start = ((), (), s32[]{:S(2)}) async-start(), calls=%async_computation.1 | async-start | bytes 393216 | tf_op jit(solution)/shard_map/psum | solution.py:153
  263.2 32.3 %copy-start.2 = (f32[128,384]{1,0:T(8,128)S(1)}, f32[128,384]{1,0:T(8,128)}, u32[]{:S(2)}) copy-start(f32[128,384]{1,0:T(8,128)} %copy.103) | copy-start | bytes 589828
  263.2 32.3 %copy-start.3 = (f32[128,384]{1,0:T(8,128)S(1)}, f32[128,384]{1,0:T(8,128)}, u32[]{:S(2)}) copy-start(f32[128,384]{1,0:T(8,128)} %copy.93) | copy-start | bytes 589828
  263.2 32.3 %copy-start.4 = (f32[128,384]{1,0:T(8,128)S(1)}, f32[128,384]{1,0:T(8,128)}, u32[]{:S(2)}) copy-start(f32[128,384]{1,0:T(8,128)} %copy.98) | copy-start | bytes 589828
  263.2 32.3 %copy-start.6 = (f32[128,384]{1,0:T(8,128)S(1)}, f32[128,384]{1,0:T(8,128)}, u32[]{:S(2)}) copy-start(f32[128,384]{1,0:T(8,128)} %copy-done.5) | copy-start | bytes 589828
  525.9 2.6 collective-permute-start.2
  527.2 4.8 collective-permute-start.3
Sparse Core Ops, SparseCore 0:
  257.2 38.2 all-reduce.20
  532.9 37.3 all-reduce.22
where the time goes:
time: 598 us; the launch traced here: 593 us
  other arithmetic  208 us (35%)
  matrix products  152 us (25%)
  local copies, waits for them, and re-layouts  121 us (20%)
  waiting for transfers between devices  71.6 us (12%)
  between operations  17.8 us (3%)
  blocking collectives  12.4 us (2%)
  starting transfers between devices  6.91 us (1%)
    add x32, other arithmetic, forward(): running + kernel_weight * (field_real * field_real + field_imag * field_i...  48.1 us
    scatter-add x64, other arithmetic, column_adjoint(): summed.at[:, b * block_cols:b * block_cols + block_cols + 2 * reach_cols]  47.9 us
    another operation x129, other arithmetic  45.9 us
    dot_general x32, matrix products, row_adjoint(): jnp.einsum('aij,bix->abjx', band_matrix, cotangent, preferred_element_typ...  43.4 us
    dot_general x32, matrix products, column_filter(): jnp.einsum('bri,poi->prbo', windows, band_matrix, preferred_element_type=...  38.8 us
    dot_general x32, matrix products, row_filter(): jnp.einsum('aij,bjx->abix', band_matrix, cfield, preferred_element_type=j...  38.4 us
    dynamic_slice x64, local copies, waits for them, and re-layouts, local(): lax.scan(forward, jnp.zeros((row_count, col_count), jnp.float32), (row_ba...  38.3 us
    psum x1, waiting for transfers between devices, local(): summed_grad = lax.psum(gradient, 'corner')  37.5 us
  transfers between devices with their start and end apart: 6, of which 3 were waited for; matrix products, arithmetic and copies ran while one was open for 10% of the time, Pallas kernels for 0%

commit v1 on v0

--- a/solution.py
+++ b/solution.py
@@ -150,7 +150,7 @@
     first_row = lax.axis_index("corner") * share_rows
     own_mask = lax.dynamic_slice_in_dim(mask, first_row, share_rows, 0)
     pixel_count = row_count * lax.axis_size("tile") * col_count
-    summed_grad = lax.psum(gradient, "corner")
+    summed_grad = jnp.sum(lax.all_gather(gradient, "corner"), axis=0)
     square = lax.psum(jnp.sum(summed_grad * summed_grad), "tile")
     own_rows = lax.dynamic_slice_in_dim(summed_grad, first_row, share_rows, 0)
     root_mean = jnp.sqrt(square / pixel_count + small_eps)

time: 598 us -> 580 us (0.970)
  waiting for transfers between devices: 71.6 us -> 33.6 us
  blocking collectives: 12.4 us -> 32.7 us
    psum x1 -> x0, waiting for transfers between devices: 37.5 us -> none  [local(): summed_grad = lax.psum(gradient, 'corner')]
    all_gather x0 -> x1, blocking collectives: none -> 17.9 us  [local(): summed_grad = jnp.sum(lax.all_gather(gradient, 'corner'), axis=0)]
    unnamed x51 -> x53, local copies, waits for them, and re-layouts: 11.5 us -> 12.4 us
  transfers between devices with their start and end apart: 6 -> 5, of which waited for: 3 -> 2; matrix products, arithmetic and copies ran while one was open for 10% -> 10% of each run, Pallas kernels for 0% -> 0%
where the time goes in v1:
time: 580 us; the launch traced here: 575 us
  other arithmetic  205 us (35%)
  matrix products  152 us (26%)
  local copies, waits for them, and re-layouts  123 us (21%)
  waiting for transfers between devices  33.6 us (6%)
  blocking collectives  32.7 us (6%)
  between operations  17.7 us (3%)
  starting transfers between devices  6.88 us (1%)
    add x32, other arithmetic, forward(): running + kernel_weight * (field_real * field_real + field_imag * field_i...  48.1 us
    another operation x129, other arithmetic  47.1 us
    scatter-add x64, other arithmetic, column_adjoint(): summed.at[:, b * block_cols:b * block_cols + block_cols + 2 * reach_cols]  45.6 us
    dot_general x32, matrix products, row_adjoint(): jnp.einsum('aij,bix->abjx', band_matrix, cotangent, preferred_element_typ...  43.4 us
    dot_general x32, matrix products, column_filter(): jnp.einsum('bri,poi->prbo', windows, band_matrix, preferred_element_type=...  38.8 us
    dynamic_slice x64, local copies, waits for them, and re-layouts, local(): lax.scan(forward, jnp.zeros((row_count, col_count), jnp.float32), (row_ba...  38.4 us
    dot_general x32, matrix products, row_filter(): jnp.einsum('aij,bjx->abix', band_matrix, cfield, preferred_element_type=j...  38.4 us
    another operation x16, local copies, waits for them, and re-layouts, toeplitz(): repeated = jnp.tile(padded, (1,) * len(leading) + (row_count,))  32.5 us
  transfers between devices with their start and end apart: 5, of which 2 were waited for; matrix products, arithmetic and copies ran while one was open for 10% of the time, Pallas kernels for 0%

profile of v1, /device:TPU:0, one launch (start us, length us, event | category | flops | bytes accessed | tf_op | source)
XLA Modules:
  0.0 574.9 jit_solution(1574689321029557206)
XLA Ops:
  9.4 3.0 collective-permute-start
  27.0 3.1 tile.39
  32.8 3.1 tile.81
  38.5 3.1 tile.83
  44.1 3.1 tile.85
  50.8 3.1 tile.87
  56.5 3.1 tile.33
  62.1 3.1 tile.35
  68.8 49.1 %while.133 = (s32[]{:T(128)}, f32[128,384]{0,1:T(8,128)}, bf16[8,2,128,384]{2,3,0,1:T(8,128)(2,1)}, f32[8]{0:T(128)S(1)}, bf16[8,2,128,256]{3,2,1,0:T(8,128)(2,1...) while((s32[]{:T(128)}, f32[128,384]{0,1:T(8,128)}, ...), condition=%wide.region_9.10_spmd.clone, body=%wide.region_8.9_spmd.clone.sunk | while | flops 203685888 | bytes 5506679 | solution.py:108
  78.1 2.3 bitcast_add_fusion.9
  84.4 2.3 bitcast_add_fusion.9
  90.6 2.3 bitcast_add_fusion.9
  96.9 2.3 bitcast_add_fusion.9
  103.1 2.3 bitcast_add_fusion.9
  109.4 2.3 bitcast_add_fusion.9
  115.6 2.3 bitcast_add_fusion.9
  121.1 49.0 %while.134 = (s32[]{:T(128)}, f32[128,384]{0,1:T(8,128)}, bf16[8,2,128,384]{2,3,0,1:T(8,128)(2,1)}, f32[8]{0:T(128)S(1)}, bf16[8,2,128,256]{3,2,1,0:T(8,128)(2,1...) while((s32[]{:T(128)}, f32[128,384]{0,1:T(8,128)}, ...), condition=%wide.region_14.15_spmd.clone, body=%wide.region_13.14_spmd.clone.sunk | while | flops 203685888 | bytes 5506679 | solution.py:108
  130.4 2.3 bitcast_add_fusion.10
  142.9 2.3 bitcast_add_fusion.10
  155.4 2.3 bitcast_add_fusion.10
  173.4 38.2 %while.135 = (s32[]{:T(128)}, f32[128,384]{0,1:T(8,128)S(1)}, bf16[8,2,128,384]{2,3,0,1:T(8,128)(2,1)}, f32[8]{0:T(128)S(1)}, bf16[8,2,128,256]{3,2,1,0:T(8,128)...) while((s32[]{:T(128)}, f32[128,384]{0,1:T(8,128)S(1)}, ...), condition=%wide.region_19.20_spmd.clone, body=%wide.region_18.19_spmd.clone.sunk | while | flops 203685888 | bytes 5506679 | solution.py:108
  213.8 38.2 %while.132 = (s32[]{:T(128)}, f32[128,384]{0,1:T(8,128)S(1)}, bf16[8,2,128,384]{2,3,0,1:T(8,128)(2,1)}, f32[8]{0:T(128)S(1)}, bf16[8,2,128,256]{3,2,0,1:T(8,128)...) while((s32[]{:T(128)}, f32[128,384]{0,1:T(8,128)S(1)}, ...), condition=%wide.region_4.5_spmd.clone, body=%wide.region_3.4_spmd.clone.sunk | while | flops 203685888 | bytes 5506679 | solution.py:108
  252.1 4.8 add_convert_fusion
  264.7 30.7 %all-reduce.20.cloned.1.call-done = bf16[128,384]{1,0:T(8,128)(2,1)} async-done(((bf16[128,384]{1,0:T(8,128)(2,1)}), bf16[128,384]{1,0:T(8,128)(2,1)}) %all-reduce.20.cloned.1.call-update) | async-done | bytes 98320 | tf_op jit(solution)/shard_map/psum | solution.py:117
  295.4 4.9 fusion.160
  300.5 57.2 %while.136 = (s32[]{:T(128)}, f32[256,384]{0,1:T(8,128)S(1)}, bf16[8,2,128,256]{3,2,0,1:T(8,128)(2,1)}, f32[8]{0:T(128)S(1)}, f32[128,384]{0,1:T(8,128)S(1)}, /*...) while((s32[]{:T(128)}, f32[256,384]{0,1:T(8,128)S(1)}, ...), condition=%wide.region_25.26_spmd.clone, body=%wide.region_23.25_spmd.clone.sunk | while | flops 203374592 | bytes 10618519 | solution.py:138
  358.7 56.9 %while.129 = (s32[]{:T(128)}, f32[256,384]{0,1:T(8,128)S(1)}, bf16[8,2,128,256]{2,3,1,0:T(8,128)(2,1)}, f32[8]{0:T(128)S(1)}, f32[128,384]{0,1:T(8,128)S(1)}, /*...) while((s32[]{:T(128)}, f32[256,384]{0,1:T(8,128)S(1)}, ...), condition=%wide.region_28.29_spmd, body=%wide.region_26.28_spmd.sunk | while | flops 203276288 | bytes 10618501 | solution.py:138
  416.7 57.0 %while.130 = (s32[]{:T(128)}, f32[256,384]{0,1:T(8,128)S(1)}, bf16[8,2,128,256]{2,3,1,0:T(8,128)(2,1)}, f32[8]{0:T(128)S(1)}, f32[128,384]{0,1:T(8,128)S(1)}, /*...) while((s32[]{:T(128)}, f32[256,384]{0,1:T(8,128)S(1)}, ...), condition=%wide.region_31.32_spmd, body=%wide.region_29.31_spmd.sunk | while | flops 203276288 | bytes 10618501 | solution.py:138
  473.8 51.8 %while.131 = (s32[]{:T(128)}, f32[256,384]{0,1:T(8,128)S(1)}, bf16[8,2,128,256]{2,3,1,0:T(8,128)(2,1)S(1)}, f32[8]{0:T(128)S(1)}, f32[128,384]{0,1:T(8,128)S(1)}...) while((s32[]{:T(128)}, f32[256,384]{0,1:T(8,128)S(1)}, ...), condition=%wide.region_34.35_spmd, body=%wide.region_32.34_spmd.sunk | while | flops 203276288 | bytes 10617993 | solution.py:138
  529.2 2.9 collective-permute-done.3
  532.3 17.9 %all-gather = f32[512,384]{0,1:T(8,128)S(1)} all-gather(f32[128,384]{0,1:T(8,128)S(1)} %pad_add_fusion), channel_id=2, replica_groups=mesh['tile'=8,'corner'=4] {'corner'}, dimensions={0}, use_global_device_ids=true | all-gather | bytes 983040 | tf_op jit(solution)/shard_map/all_gather | solution.py:153
  551.7 14.8 %psum.15 = f32[]{:T(128)} all-reduce(f32[]{:T(128)} %multiply_reduce_fusion), channel_id=1, replica_groups=mesh['tile'=8,'corner'=4] {'tile'}, use_global_device_ids=true, to_apply=%region_37.38 | all-reduce | flops 1 | bytes 8 | tf_op jit(solution)/shard_map/psum | solution.py:154
  (752 shorter events, 430.1 us)
Async XLA Ops:
  7.2 288.2 %all-reduce.20.cloned.1.call-start = ((), (), s32[]{:S(2)}) async-start(), calls=%async_computation | async-start | bytes 196608 | tf_op jit(solution)/shard_map/psum | solution.py:117
  8.2 0.6 copy-start.7
  9.4 57.1 %collective-permute-start = (bf16[64,384]{1,0:T(8,128)(2,1)}, bf16[64,384]{1,0:T(8,128)(2,1)}, u32[]{:S(2)}, u32[]{:S(2)}) collective-permute-start(bf16[64,384]{1,0:T(8,128)(2,1)} %get-tuple-element.1632), channel_id=1, source_target_pairs={{0,4},{4,8},{8,12},{12,16},{16,20},{20,24},{24,28},{1,5},{5,9},{9,... | collective-permute-start | bytes 147464 | tf_op jit(solution)/shard_map/ppermute | solution.py:21
  12.4 54.1 %collective-permute-start.1 = (bf16[64,384]{1,0:T(8,128)(2,1)}, bf16[64,384]{1,0:T(8,128)(2,1)}, u32[]{:S(2)}, u32[]{:S(2)}) collective-permute-start(bf16[64,384]{1,0:T(8,128)(2,1)} %get-tuple-element.1633), channel_id=1, source_target_pairs={{4,0},{8,4},{12,8},{16,12},{20,16},{24,20},{28,24},{5,1},{9,5},{13... | collective-permute-start | bytes 147464 | tf_op jit(solution)/shard_map/ppermute | solution.py:22
  30.1 1.3 copy-start.13
  35.9 1.3 copy-start.12
  41.6 1.2 copy-start.11
  47.3 1.0 copy-start
  48.3 1.2 copy-start.10
  53.9 1.2 copy-start.9
  65.3 1.2 copy-start.8
  65.3 3.5 copy-start.15
  117.9 3.2 copy-start.14
  211.6 2.3 copy-start.16
  252.1 6.7 %copy-start.5 = (f32[128,384]{1,0:T(8,128)}, f32[128,384]{1,0:T(8,128)S(1)}, u32[]{:S(2)}) copy-start(f32[128,384]{1,0:T(8,128)S(1)} %copy.82) | copy-start | bytes 589828
  261.2 1.7 copy-start.1
  263.0 32.4 %copy-start.2 = (f32[128,384]{1,0:T(8,128)S(1)}, f32[128,384]{1,0:T(8,128)}, u32[]{:S(2)}) copy-start(f32[128,384]{1,0:T(8,128)} %copy.87) | copy-start | bytes 589828
  263.0 32.4 %copy-start.3 = (f32[128,384]{1,0:T(8,128)S(1)}, f32[128,384]{1,0:T(8,128)}, u32[]{:S(2)}) copy-start(f32[128,384]{1,0:T(8,128)} %copy.92) | copy-start | bytes 589828
  263.0 32.4 %copy-start.4 = (f32[128,384]{1,0:T(8,128)S(1)}, f32[128,384]{1,0:T(8,128)}, u32[]{:S(2)}) copy-start(f32[128,384]{1,0:T(8,128)} %copy.97) | copy-start | bytes 589828
  263.0 32.4 %copy-start.6 = (f32[128,384]{1,0:T(8,128)S(1)}, f32[128,384]{1,0:T(8,128)}, u32[]{:S(2)}) copy-start(f32[128,384]{1,0:T(8,128)} %copy-done.5) | copy-start | bytes 589828
  525.8 3.4 collective-permute-start.2
  527.1 5.0 collective-permute-start.3
Sparse Core Ops, SparseCore 0:
  257.1 38.3 all-reduce.19
